TPU v7x, 32 devices: a whole 2x2x4 slice. The times are simulated.
32 devices in a mesh: gx: 8 (over z, x), gy: 2 (over y), gz: 2 (over core).
Axes of the slice: x: 2, y: 2, z: 4, core: 2. Of those that a mesh axis runs over, the one named last changes fastest.
Arguments:
- velocity: float32 [3, 32, 64, 1024], P(None, 'gz', 'gx', 'gy'), may hold values from -6 to 6
- column_state: float32 [2, 64, 64, 1024], P(None, None, 'gx', ('gy', 'gz')), may hold values from -4 to 4
- height_index: int32 [64, 1024], P('gx', 'gy'), may hold values from 1 to 8
- rotor_mask: int32 [32, 64, 1024], P('gz', 'gx', 'gy'), may hold values from 0 to 8, as said below
- thrust: float32 [8], replicated, may hold values from 1 to 4
Outputs:
- advanced: float32 [3, 32, 64, 1024], P(None, 'gz', 'gx', 'gy')
- fresh_state: float32 [2, 64, 64, 1024], P(None, None, 'gx', ('gy', 'gz'))
Inputs may be any that keep to these rules, and one draw needn't show every extreme that they name: `height_index`: each ground face's sampling layer, counted from the ground. `rotor_mask`: cells holding k + 1 form rotor k's disk of radius 6 cells; all 8 disks lie in one z layer between 2 and 9.
All inputs are finite; a program needn't handle non-finite values.
Results may differ from a plain program's by a relative error of at most 0.000034.
Values sent between devices are 32-bit elements; how exact they have to be, the bound alone decides.
A program may use at most 64 MiB of HBM per device.

v0:
```python
import math

import jax
import jax.numpy as jnp
from jax import lax
from jax.sharding import PartitionSpec as P

LEVELS = 8


time_step = 0.1
viscosity = 0.02
smag_coeff = 0.0289
karman = 0.41
wall_step = 0.05
stretch = 3.0


def with_halo(block, sides, width, periodic):
    for axis, dim in sides:
        count = lax.axis_size(axis)
        forward = [(i, i + 1) for i in range(count - 1)]
        if periodic:
            forward.append((count - 1, 0))
        backward = [(target, source) for source, target in forward]
        low = lax.ppermute(
            lax.slice_in_dim(block, block.shape[dim] - width, None, axis=dim), axis, forward
        )
        high = lax.ppermute(lax.slice_in_dim(block, 0, width, axis=dim), axis, backward)
        block = jnp.concatenate([low, block, high], axis=dim)
    return block


def sample(lowest, height_index):
    picked = jnp.zeros_like(lowest[:, 0])
    for layer_z in range(1, lowest.shape[1]):
        picked = picked + jnp.where((height_index == layer_z)[None], lowest[:, layer_z], 0.0)
    return picked


def column_step(state, top_speed, sample_height):
    count = state.shape[1]
    ladder = jnp.arange(count, dtype=jnp.float32) / (count - 1)
    spacing = (jnp.exp(stretch * ladder) - 1.0) / (math.exp(stretch) - 1.0)
    heights = spacing.reshape((count,) + (1,) * sample_height.ndim) * sample_height[None]
    spacing_gap = heights[1:] - heights[:-1]
    middle = 0.5 * (heights[1:] + heights[:-1])
    differ = state[:, 1:] - state[:, :-1]
    shear_rate = jnp.sqrt(differ[0] * differ[0] + differ[1] * differ[1] + 1e-06) / spacing_gap
    eddy_visc = viscosity + (karman * middle) ** 2 * shear_rate
    conduct = eddy_visc / spacing_gap
    volume = 0.5 * (spacing_gap[1:] + spacing_gap[:-1]) / wall_step
    band_low = -conduct[:-1]
    band_up = -conduct[1:]
    band_mid = volume + conduct[:-1] + conduct[1:]
    source = volume[None] * state[:, 1:-1]
    source = source.at[:, -1].add(conduct[-1][None] * top_speed)

    def forward(pair_in, entries):
        prev_c, prev_d = pair_in
        low_e, mid_e, up_e, src_e = entries
        denom = mid_e - low_e * prev_c
        cur_c = up_e / denom
        cur_d = (src_e - low_e[None] * prev_d) / denom[None]
        return ((cur_c, cur_d), (cur_c, cur_d))

    start_pair = (jnp.zeros_like(sample_height), jnp.zeros_like(top_speed))
    _, (coef_c, coef_d) = lax.scan(
        forward, start_pair, (band_low, band_mid, band_up, jnp.moveaxis(source, 1, 0)), unroll=True
    )

    def backward(later, entries):
        cur_c, cur_d = entries
        value = cur_d - cur_c[None] * later
        return (value, value)

    _, solved = lax.scan(
        backward, jnp.zeros_like(top_speed), (coef_c, coef_d), reverse=True, unroll=True
    )
    solved = jnp.moveaxis(solved, 0, 1)
    fresh = jnp.concatenate([jnp.zeros_like(solved[:, :1]), solved, top_speed[:, None]], axis=1)
    stress = conduct[0][None] * solved[:, 0]
    return (fresh, stress)


def advance(velocity, planar, stacked, stress, bottom_flag, rotor_mask, thrust):
    x_next = planar[:, :, 2:, 1:-1]
    x_prev = planar[:, :, :-2, 1:-1]
    y_next = planar[:, :, 1:-1, 2:]
    y_prev = planar[:, :, 1:-1, :-2]
    z_next = stacked[:, 2:]
    z_prev = stacked[:, :-2]
    grad_x = 0.5 * (x_next - x_prev)
    grad_y = 0.5 * (y_next - y_prev)
    grad_z = 0.5 * (z_next - z_prev)
    strain_xy = 0.5 * (grad_y[0] + grad_x[1])
    strain_xz = 0.5 * (grad_z[0] + grad_x[2])
    strain_yz = 0.5 * (grad_z[1] + grad_y[2])
    diag_part = grad_x[0] * grad_x[0] + grad_y[1] * grad_y[1] + grad_z[2] * grad_z[2]
    cross_part = strain_xy * strain_xy + strain_xz * strain_xz + strain_yz * strain_yz
    strain_norm = jnp.sqrt(2.0 * diag_part + 4.0 * cross_part + 1e-06)
    viscous = viscosity + smag_coeff * strain_norm
    laplace = x_next + x_prev + y_next + y_prev + z_next + z_prev - 6.0 * velocity
    advect = 0.5 * (x_next * x_next[0:1] - x_prev * x_prev[0:1])
    advect = advect + 0.5 * (y_next * y_next[1:2] - y_prev * y_prev[1:2])
    advect = advect + 0.5 * (z_next * z_next[2:3] - z_prev * z_prev[2:3])
    tendency = viscous[None] * laplace - advect
    wall_term = viscous[0][None] * velocity[:2, 0] - stress
    tendency = tendency.at[:2, 0].add(bottom_flag * wall_term)
    thrust_force = jnp.zeros_like(velocity[2])
    for rotor_id in range(thrust.shape[0]):
        thrust_force = thrust_force + jnp.where(rotor_mask == rotor_id + 1, thrust[rotor_id], 0.0)
    tendency = tendency.at[2].add(-thrust_force)
    return velocity + time_step * tendency


def lift(ground):
    lead_dims = ground.shape[:-1]
    span_count = lax.axis_size("gy")
    core_count = lax.axis_size("gz")
    width_ground = ground.shape[-1]
    block_len = width_ground // (span_count * core_count)
    flat = ground.reshape(-1, width_ground)
    arrived = lax.all_to_all(flat, ("gy", "gz"), split_axis=1, concat_axis=1, tiled=True)
    arrived = arrived.reshape(-1, span_count, core_count, block_len)[:, :, 0, :]
    ordered = jnp.swapaxes(arrived, 1, 2)
    return ordered.reshape(lead_dims + (span_count * block_len,))


def lower(columns_in):
    lead_dims = columns_in.shape[:-1]
    span_count = lax.axis_size("gy")
    core_count = lax.axis_size("gz")
    width_cols = columns_in.shape[-1]
    block_len = width_cols // span_count
    width_ground = width_cols * core_count
    back_order = jnp.swapaxes(columns_in.reshape(-1, block_len, span_count), 1, 2)
    empty_slots = jnp.zeros(back_order.shape[:2] + (core_count - 1, block_len), back_order.dtype)
    slots = jnp.concatenate([back_order[:, :, None, :], empty_slots], axis=2)
    arrived = lax.all_to_all(
        slots.reshape(-1, width_ground), ("gy", "gz"), split_axis=1, concat_axis=1, tiled=True
    )
    return arrived.reshape(lead_dims + (width_ground,))


def local(velocity, column_state, height_index, rotor_mask, thrust):
    bottom_flag = (lax.axis_index("gz") == 0).astype(jnp.float32)
    top_speed = sample(velocity[:2, : LEVELS + 1], height_index)
    sample_height = height_index.astype(jnp.float32) + 0.5
    ground_state = lower(column_state)
    fresh_ground, stress = column_step(ground_state, top_speed, sample_height)
    fresh_state = lift(fresh_ground)
    planar = with_halo(velocity, (("gx", 2), ("gy", 3)), 1, True)
    stacked = with_halo(velocity, (("gz", 1),), 1, False)
    advanced = advance(velocity, planar, stacked, stress, bottom_flag, rotor_mask, thrust)
    return (advanced, fresh_state)


def solution(mesh):
    in_specs = (
        P(None, "gz", "gx", "gy"),
        P(None, None, "gx", ("gy", "gz")),
        P("gx", "gy"),
        P("gz", "gx", "gy"),
        P(),
    )
    out_specs = (P(None, "gz", "gx", "gy"), P(None, None, "gx", ("gy", "gz")))
    return jax.shard_map(local, mesh=mesh, in_specs=in_specs, out_specs=out_specs, check_vma=False)
```

profile of v0, /device:TPU:0, one launch (start us, length us, event | category | flops | bytes accessed | tf_op | source)
XLA Modules:
  0.0 164.7 jit_solution(9760664101878547590)
XLA Ops:
  0.6 0.8 fusion.466
  1.5 2.3 %collective-permute-start.5 = (f32[3,1,8,512]{3,2,0,1:T(8,128)S(1)}, f32[3,1,8,512]{3,2,0,1:T(8,128)S(1)}, u32[]{:S(2)}, u32[]{:S(2)}) collective-permute-start(f32[3,1,8,512]{3,2,0,1:T(8,128)S(1)} %get-tuple-element.317), channel_id=1, source_target_pairs={{0,1},{2,3},{4,5},{6,7},{8,9},{10,11},{12,13},{14,15},{16,17},{18,... | collective-permute-start | bytes 147464 | tf_op jit(solution)/shard_map/ppermute | solution.py:26
  3.8 1.3 collective-permute-start.4
  5.1 1.6 fusion.465
  6.7 5.4 %collective-permute-start = (f32[3,16,1,512]{3,2,0,1:T(1,128)S(1)}, f32[3,16,1,512]{3,2,0,1:T(1,128)S(1)}, u32[]{:S(2)}, u32[]{:S(2)}) collective-permute-start(f32[3,16,1,512]{3,2,0,1:T(1,128)S(1)} %get-tuple-element.312), channel_id=1, source_target_pairs={{4,0},{8,4},{12,8},{16,12},{20,16},{24,20},{28,24},{0,28},{5,1},{9... | collective-permute-start | bytes 294920 | tf_op jit(solution)/shard_map/ppermute | solution.py:29
  12.1 14.2 %copy.308 = f32[2,64,8,256]{2,1,0,3:T(8,128)} copy(f32[2,64,8,256]{3,2,1,0:T(8,128)} %param.12) | data formatting | bytes 2097152 | tf_op args[1]
  26.3 12.2 %reshape.217 = f32[1024,128,2]{0,2,1:T(2,128)S(1)} reshape(f32[2,64,8,256]{2,1,0,3:T(8,128)} %copy.308) | data formatting | bytes 2097152 | tf_op jit(solution)/shard_map/reshape | solution.py:137
  38.6 0.5 copy.451
  39.1 1.5 concatenate.45.clone
  40.5 3.9 %all-to-all-start = ((f32[1024,4,128]{2,0,1:T(8,128)}), f32[1024,4,128]{2,0,1:T(8,128)S(1)}, u32[]{:S(2)}, u32[]{:S(2)}) async-start(f32[1024,4,128]{2,0,1:T(8,128)} %bitcast.2396), calls=%async_computation | async-start | bytes 4194304 | tf_op jit(solution)/shard_map/all_to_all | solution.py:140
  44.5 1.1 broadcast_multiply_fusion
  45.7 0.7 fusion.467
  46.3 0.9 copy.383
  47.3 1.3 constant_dynamic-update-slice_fusion
  48.6 1.2 subtract_multiply_fusion
  49.9 0.7 slice_bitcast_fusion.1
  50.6 0.7 slice_bitcast_fusion.2
  51.3 1.2 pad_maximum_fusion.3
  52.5 1.8 %collective-permute-start.2 = (f32[3,16,10,1]{3,2,0,1:T(8,128)}, f32[3,16,10,1]{3,2,0,1:T(8,128)S(1)}, u32[]{:S(2)}, u32[]{:S(2)}) collective-permute-start(f32[3,16,10,1]{3,2,0,1:T(8,128)} %get-tuple-element.307), channel_id=1, source_target_pairs={{2,0},{0,2},{3,1},{1,3},{6,4},{4,6},{7,5},{5,7},{10,8},{8,10},{11,... | collective-permute-start | bytes 5768 | tf_op jit(solution)/shard_map/ppermute | solution.py:29
  54.5 3.1 %dynamic-update-slice.76 = f32[3,16,9,512]{3,2,0,1:T(8,128)} dynamic-update-slice(f32[3,16,9,512]{3,2,0,1:T(8,128)} %get-tuple-element.313, f32[3,16,1,512]{3,2,0,1:T(1,128)S(1)} %collective-permute-done, s32[]{} %constant.163, s32[]{} %constant.163, s32[]{} %constant.171, s32[]{} %constant.163) | dynamic-update-slice | bytes 196612 | tf_op jit(solution)/shard_map/concatenate | solution.py:30
  57.6 1.8 %slice_bitcast_fusion.3 = f32[16,8,512]{2,1,0:T(8,128)} fusion(f32[3,16,9,512]{3,2,0,1:T(8,128)} %dynamic-update-slice.76), kind=kLoop, calls=%fused_computation.48 | loop fusion | bytes 524288 | tf_op jit(solution)/shard_map/mul | solution.py:104
  59.4 19.5 %collective-permute-done.2 = f32[3,16,10,1]{3,2,0,1:T(8,128)S(1)} collective-permute-done((f32[3,16,10,1]{3,2,0,1:T(8,128)}, f32[3,16,10,1]{3,2,0,1:T(8,128)S(1)}, u32[]{:S(2)}, u32[]{:S(2)}) %collective-permute-start.2) | collective-permute-done | bytes 1952 | tf_op jit(solution)/shard_map/ppermute | solution.py:29
  78.9 8.4 %collective-permute-done.3 = f32[3,16,10,1]{3,2,0,1:T(8,128)} collective-permute-done((f32[3,16,10,1]{3,2,0,1:T(8,128)}, f32[3,16,10,1]{3,2,0,1:T(8,128)}, u32[]{:S(2)}, u32[]{:S(2)}) %collective-permute-start.3) | collective-permute-done | bytes 1952 | tf_op jit(solution)/shard_map/ppermute | solution.py:26
  87.3 2.6 %subtract_multiply_fusion.2 = (f32[3,16,8,512]{3,2,0,1:T(8,128)S(1)}, f32[3,16,8,512]{3,2,0,1:T(8,128)S(1)}) fusion(f32[3,16,9,512]{3,2,0,1:T(8,128)} %dynamic-update-slice.76, f32[3,16,1,512]{3,2,0,1:T(1,128)S(1)} %collective-permute-done.1, f32[3,16,1,512]{3,2,0,1:T(1,128)S(1)} %collective-permute-done, f32[3,16,10,1]{3,2,0,1:T(8,128)} %collective-permute-done.3, ...), kind=kLoop, calls=%fused_computation.29 | loop fusion | flops 2162688 | bytes 3346176 | tf_op jit(solution)/shard_map/mul | solution.py:93
  89.9 1.0 fusion.22
  90.9 2.7 %copy.310 = f32[1024,4,128]{2,1,0:T(4,128)} copy(f32[1024,4,128]{2,0,1:T(8,128)S(1)} %all-to-all-done) | data formatting | bytes 4194304 | tf_op jit(solution)/shard_map/all_to_all | solution.py:140
  93.6 2.1 %reshape.218 = f32[2,64,8,512]{3,2,1,0:T(8,128)S(1)} reshape(f32[1024,4,128]{2,1,0:T(4,128)} %copy.310) | data formatting | bytes 4194304 | tf_op jit(solution)/shard_map/reshape | solution.py:143
  95.9 1.0 copy-done.1
  96.9 0.7 fusion.7
  97.6 0.6 add_add_fusion
  98.2 0.4 fusion.256
  100.1 0.7 constant_dynamic-update-slice_fusion.66
  101.4 0.9 constant_dynamic-update-slice_fusion.23
  102.8 1.1 copy-done.7
  104.1 1.7 %all_to_all.14 = f32[1024,4,128]{2,1,0:T(4,128)} reshape(f32[2,64,8,512]{3,2,1,0:T(8,128)S(1)} %copy.384) | data formatting | bytes 4194304 | tf_op jit(solution)/shard_map/all_to_all | solution.py:124
  105.8 3.1 %copy.385 = f32[1024,4,128]{2,0,1:T(8,128)} copy(f32[1024,4,128]{2,1,0:T(4,128)} %all_to_all.14) | data formatting | bytes 4194304 | tf_op jit(solution)/shard_map/all_to_all | solution.py:124
  108.9 3.8 %all-to-all-start.1 = ((f32[1024,4,128]{2,0,1:T(8,128)}), f32[1024,4,128]{2,0,1:T(8,128)S(1)}, u32[]{:S(2)}, u32[]{:S(2)}) async-start(f32[1024,4,128]{2,0,1:T(8,128)} %copy.385), calls=%async_computation.1 | async-start | bytes 4194304 | tf_op jit(solution)/shard_map/all_to_all | solution.py:124
  112.8 0.9 slice_bitcast_fusion.64
  113.6 1.3 fusion.12
  114.9 4.4 %multiply_subtract_fusion = f32[3,16,8,512]{3,2,0,1:T(8,128)S(1)} fusion(f32[3,16,8,512]{3,2,0,1:T(8,128)} %copy.383, f32[3,17,8,512]{3,2,0,1:T(8,128)} %copy-done.5, f32[3,17,8,512]{3,2,0,1:T(8,128)S(1)} %copy-done.3, f32[3,16,9,512]{3,2,0,1:T(8,128)S(1)} %copy-done.4, f32[3,16,10,1]{3,2,0,1:T(8,128)S(1)} %collective-permute-done.2, ...), kind=kLoop, calls=%fused_computation.26 | loop fusion | flops 5505024 | bytes 5967616 | tf_op jit(solution)/shard_map/sub | solution.py:107
  119.3 0.8 fusion.34
  120.1 5.4 %fusion.10 = f32[3,16,8,512]{3,2,0,1:T(8,128)S(1)} fusion(f32[3,16,8,512]{3,2,0,1:T(8,128)S(1)} %fusion.34, s32[16,8,512]{2,1,0:T(8,128)S(1)} %copy-done.8, f32[]{:T(128)} %bitcast.378, f32[]{:T(128)} %bitcast.377, f32[]{:T(128)} %bitcast.376, f32[]{:T(128)} %bitcast.375, f32[]{:T(128)} %bitcast.374, f32[]{:T(128)} %bitcast.373, f32[]{:T(128)} %bitcast.372, ...), kind=kLoop, calls=%fused_computation.35 | loop fusion | flops 1638400 | bytes 786464 | tf_op jit(solution)/shard_map/scatter-add | solution.py:113
  125.7 0.9 copy.387
  126.6 11.6 %all-to-all-done.1 = f32[1024,4,128]{2,0,1:T(8,128)S(1)} async-done(((f32[1024,4,128]{2,0,1:T(8,128)}), f32[1024,4,128]{2,0,1:T(8,128)S(1)}, u32[]{:S(2)}, u32[]{:S(2)}) %all-to-all-start.1) | async-done | bytes 2097184 | tf_op jit(solution)/shard_map/all_to_all | solution.py:124
  138.2 1.0 slice_bitcast_fusion
  139.2 1.6 copy.386
  140.8 11.3 %reshape.221 = f32[2,64,8,256]{2,1,0,3:T(8,128)} reshape(f32[1024,128,2]{0,2,1:T(2,128)S(1)} %copy.386) | data formatting | bytes 2097152 | tf_op jit(solution)/shard_map/reshape | solution.py:127
  152.1 12.6 %copy.388 = f32[2,64,8,256]{3,2,1,0:T(8,128)} copy(f32[2,64,8,256]{2,1,0,3:T(8,128)} %reshape.221) | data formatting | bytes 2097152
  (132 shorter events, 2.8 us)
Async XLA Ops:
  1.5 45.8 %collective-permute-start.5 = (f32[3,1,8,512]{3,2,0,1:T(8,128)S(1)}, f32[3,1,8,512]{3,2,0,1:T(8,128)S(1)}, u32[]{:S(2)}, u32[]{:S(2)}) collective-permute-start(f32[3,1,8,512]{3,2,0,1:T(8,128)S(1)} %get-tuple-element.317), channel_id=1, source_target_pairs={{0,1},{2,3},{4,5},{6,7},{8,9},{10,11},{12,13},{14,15},{16,17},{18,... | collective-permute-start | bytes 147464 | tf_op jit(solution)/shard_map/ppermute | solution.py:26
  3.8 44.8 %collective-permute-start.4 = (f32[3,1,8,512]{3,2,0,1:T(8,128)S(1)}, f32[3,1,8,512]{3,2,0,1:T(8,128)S(1)}, u32[]{:S(2)}, u32[]{:S(2)}) collective-permute-start(f32[3,1,8,512]{3,2,0,1:T(8,128)S(1)} %get-tuple-element.316), channel_id=1, source_target_pairs={{1,0},{3,2},{5,4},{7,6},{9,8},{11,10},{13,12},{15,14},{17,16},{19,... | collective-permute-start | bytes 147464 | tf_op jit(solution)/shard_map/ppermute | solution.py:29
  6.7 44.6 %collective-permute-start = (f32[3,16,1,512]{3,2,0,1:T(1,128)S(1)}, f32[3,16,1,512]{3,2,0,1:T(1,128)S(1)}, u32[]{:S(2)}, u32[]{:S(2)}) collective-permute-start(f32[3,16,1,512]{3,2,0,1:T(1,128)S(1)} %get-tuple-element.312), channel_id=1, source_target_pairs={{4,0},{8,4},{12,8},{16,12},{20,16},{24,20},{28,24},{0,28},{5,1},{9... | collective-permute-start | bytes 294920 | tf_op jit(solution)/shard_map/ppermute | solution.py:29
  12.1 39.2 %collective-permute-start.1 = (f32[3,16,1,512]{3,2,0,1:T(1,128)S(1)}, f32[3,16,1,512]{3,2,0,1:T(1,128)S(1)}, u32[]{:S(2)}, u32[]{:S(2)}) collective-permute-start(f32[3,16,1,512]{3,2,0,1:T(1,128)S(1)} %get-tuple-element.311), channel_id=1, source_target_pairs={{0,4},{4,8},{8,12},{12,16},{16,20},{20,24},{24,28},{28,0},{1,5},{5... | collective-permute-start | bytes 294920 | tf_op jit(solution)/shard_map/ppermute | solution.py:26
  40.5 4.0 %copy-start.9 = (s32[8,512]{1,0:T(8,128)S(1)}, s32[8,512]{1,0:T(8,128)}, u32[]{:S(2)}) copy-start(s32[8,512]{1,0:T(8,128)} %param.13) | copy-start | bytes 49156
  40.5 5.1 %copy-start.10 = (f32[8]{0:T(128)S(1)}, f32[8]{0:T(128)}, u32[]{:S(2)}) copy-start(f32[8]{0:T(128)} %param.15) | copy-start | bytes 100
  40.5 5.8 %copy-start = (f32[3,16,8,512]{3,2,1,0:T(8,128)S(1)}, f32[3,16,8,512]{3,2,1,0:T(8,128)}, u32[]{:S(2)}) copy-start(f32[3,16,8,512]{3,2,1,0:T(8,128)} %param.11) | copy-start | bytes 2359300
  40.5 50.4 %all-to-all-start = ((f32[1024,4,128]{2,0,1:T(8,128)}), f32[1024,4,128]{2,0,1:T(8,128)S(1)}, u32[]{:S(2)}, u32[]{:S(2)}) async-start(f32[1024,4,128]{2,0,1:T(8,128)} %bitcast.2396), calls=%async_computation | async-start | bytes 4194304 | tf_op jit(solution)/shard_map/all_to_all | solution.py:140
  48.6 3.9 %copy-start.5 = (f32[3,17,8,512]{3,2,0,1:T(8,128)}, f32[3,17,8,512]{3,2,0,1:T(8,128)S(1)}, u32[]{:S(2)}) copy-start(f32[3,17,8,512]{3,2,0,1:T(8,128)S(1)} %get-tuple-element.315) | copy-start | bytes 2506756
  48.6 3.9 %copy-start.2 = (f32[3,17,8,512]{3,2,0,1:T(8,128)}, f32[3,17,8,512]{3,2,0,1:T(8,128)S(1)}, u32[]{:S(2)}) copy-start(f32[3,17,8,512]{3,2,0,1:T(8,128)S(1)} %constant_dynamic-update-slice_fusion.1) | copy-start | bytes 2506756
  52.5 26.4 %collective-permute-start.2 = (f32[3,16,10,1]{3,2,0,1:T(8,128)}, f32[3,16,10,1]{3,2,0,1:T(8,128)S(1)}, u32[]{:S(2)}, u32[]{:S(2)}) collective-permute-start(f32[3,16,10,1]{3,2,0,1:T(8,128)} %get-tuple-element.307), channel_id=1, source_target_pairs={{2,0},{0,2},{3,1},{1,3},{6,4},{4,6},{7,5},{5,7},{10,8},{8,10},{11,... | collective-permute-start | bytes 5768 | tf_op jit(solution)/shard_map/ppermute | solution.py:29
  54.3 33.0 %collective-permute-start.3 = (f32[3,16,10,1]{3,2,0,1:T(8,128)}, f32[3,16,10,1]{3,2,0,1:T(8,128)}, u32[]{:S(2)}, u32[]{:S(2)}) collective-permute-start(f32[3,16,10,1]{3,2,0,1:T(8,128)} %get-tuple-element.306), channel_id=1, source_target_pairs={{0,2},{2,0},{1,3},{3,1},{4,6},{6,4},{5,7},{7,5},{8,10},{10,8},{9,1... | collective-permute-start | bytes 5768 | tf_op jit(solution)/shard_map/ppermute | solution.py:26
  59.4 30.5 %copy-start.6 = (f32[3,16,8,512]{3,2,0,1:T(8,128)S(1)}, f32[3,16,8,512]{3,2,0,1:T(8,128)}, u32[]{:S(2)}) copy-start(f32[3,16,8,512]{3,2,0,1:T(8,128)} %subtract_multiply_fusion) | copy-start | bytes 2359300
  95.7 1.2 copy-start.1
  102.6 1.3 copy-start.7
  108.9 29.3 %all-to-all-start.1 = ((f32[1024,4,128]{2,0,1:T(8,128)}), f32[1024,4,128]{2,0,1:T(8,128)S(1)}, u32[]{:S(2)}, u32[]{:S(2)}) async-start(f32[1024,4,128]{2,0,1:T(8,128)} %copy.385), calls=%async_computation.1 | async-start | bytes 4194304 | tf_op jit(solution)/shard_map/all_to_all | solution.py:124
  112.7 2.2 %copy-start.3 = (f32[3,17,8,512]{3,2,0,1:T(8,128)S(1)}, f32[3,17,8,512]{3,2,0,1:T(8,128)}, u32[]{:S(2)}) copy-start(f32[3,17,8,512]{3,2,0,1:T(8,128)} %copy-done.2) | copy-start | bytes 2506756
  112.8 2.2 %copy-start.4 = (f32[3,16,9,512]{3,2,0,1:T(8,128)S(1)}, f32[3,16,9,512]{3,2,0,1:T(8,128)}, u32[]{:S(2)}) copy-start(f32[3,16,9,512]{3,2,0,1:T(8,128)} %dynamic-update-slice.76) | copy-start | bytes 2654212
  114.9 5.2 %copy-start.8 = (s32[16,8,512]{2,1,0:T(8,128)S(1)}, s32[16,8,512]{2,1,0:T(8,128)}, u32[]{:S(2)}) copy-start(s32[16,8,512]{2,1,0:T(8,128)} %param.14) | copy-start | bytes 786436
where the time goes:
time: 166 us; the launch traced here: 165 us
  local copies, waits for them, and re-layouts  80.5 us (48%)
  waiting for transfers between devices  39.5 us (24%)
  other arithmetic  24.3 us (15%)
  starting transfers between devices  18.8 us (11%)
    unnamed x58, local copies, waits for them, and re-layouts  32.9 us
    ppermute x3, waiting for transfers between devices, with_halo(): lax.ppermute(lax.slice_in_dim(block, 0, width, axis=dim), axis, backward)  19.5 us
    reshape x1, local copies, waits for them, and re-layouts, lower(): columns_in.reshape(-1, block_len, span_count)  12.2 us
    all_to_all x1, waiting for transfers between devices, lift(): lax.all_to_all(flat, ('gy', 'gz'), split_axis=1, concat_axis=1, tiled=True)  11.6 us
    reshape x1, local copies, waits for them, and re-layouts, lift(): return ordered.reshape(lead_dims + (span_count * block_len,))  11.3 us
    ppermute x3, starting transfers between devices, with_halo(): lax.ppermute(lax.slice_in_dim(block, 0, width, axis=dim), axis, backward)  8.51 us
    ppermute x3, waiting for transfers between devices, with_halo(): lax.ppermute(lax.slice_in_dim(block, block.shape[dim] - width, None, axis...  8.37 us
    scatter-add x1, other arithmetic, advance(): tendency = tendency.at[2].add(-thrust_force)  5.35 us
  transfers between devices with their start and end apart: 8, of which 3 were waited for; matrix products, arithmetic and copies ran while one was open for 37% of the time, Pallas kernels for 0%

commit v1 on v0

v1 whole, which is shorter than its diff:
```python
import functools
import math

import jax
import jax.numpy as jnp
import numpy as np
from jax import lax
from jax.experimental import pallas as pl
from jax.experimental.pallas import tpu as pltpu
from jax.sharding import PartitionSpec as P

LEVELS = 8
LANES = 128
MESH = pl.DeviceIdType.MESH
CHUNKS = 4

time_step = 0.1
viscosity = 0.02
smag_coeff = 0.0289
karman = 0.41
wall_step = 0.05
stretch = 3.0


def column_constants(points):
    ladder = np.arange(points, dtype=np.float64) / (points - 1)
    spacing = (np.exp(stretch * ladder) - 1.0) / (math.exp(stretch) - 1.0)
    gap = spacing[1:] - spacing[:-1]
    middle = 0.5 * (spacing[1:] + spacing[:-1])
    laminar = viscosity / gap
    eddy = (karman * middle / gap) ** 2
    volume = np.zeros_like(gap)
    volume[1:] = 0.5 * (gap[1:] + gap[:-1]) / wall_step
    return [[float(np.float32(v)) for v in row] for row in (laminar, eddy, volume)]


def kernel(
    sizes,
    v_hbm, s_hbm, h_hbm, m_hbm, thrust_ref, tab_ref,
    adv_ref, fresh_ref,
    v, s, h, mask, eddy, coef_e, coef_f,
    xlo, xhi, zhalo, ypack_lo, ypack_hi, ylo, yhi,
    stage, tops, back, walls, plane,
    load_sem, x_send, x_recv, y_send, y_recv, z_send, z_recv, t_send, t_recv, w_send, w_recv,
):
    n_gx, n_gy, n_gz, layers, rows, width, points, cols = sizes
    group = n_gy * n_gz
    block = width // group
    tiles = width // LANES
    gx, gy, gz = lax.axis_index("gx"), lax.axis_index("gy"), lax.axis_index("gz")
    me = gy * n_gz + gz
    left, right = lax.rem(gx + n_gx - 1, n_gx), lax.rem(gx + 1, n_gx)
    below, above = lax.rem(gy + n_gy - 1, n_gy), lax.rem(gy + 1, n_gy)
    at_wall = gz == 0

    loads = [
        pltpu.make_async_copy(h_hbm, h, load_sem.at[0]),
        pltpu.make_async_copy(
            v_hbm.at[pl.ds(0, 2), pl.ds(0, LEVELS + 1)], v.at[pl.ds(0, 2), pl.ds(0, LEVELS + 1)], load_sem.at[1]
        ),
        pltpu.make_async_copy(
            v_hbm.at[pl.ds(0, 2), pl.ds(LEVELS + 1, layers - LEVELS - 1)],
            v.at[pl.ds(0, 2), pl.ds(LEVELS + 1, layers - LEVELS - 1)],
            load_sem.at[2],
        ),
        pltpu.make_async_copy(v_hbm.at[2], v.at[2], load_sem.at[3]),
        pltpu.make_async_copy(s_hbm, s, load_sem.at[4]),
        pltpu.make_async_copy(m_hbm.at[pl.ds(2, 8)], mask, load_sem.at[5]),
    ]
    for load in loads:
        load.start()

    barrier = pltpu.get_barrier_semaphore()
    for side in (left, right):
        pl.semaphore_signal(barrier, inc=1, device_id=(side, gy, gz), device_id_type=MESH)
    for d in range(1, group):
        r = lax.rem(me + d, group)
        pl.semaphore_signal(barrier, inc=1, device_id=(gx, r // n_gz, r % n_gz), device_id_type=MESH)

    loads[0].wait()
    loads[1].wait()

    @pl.when(at_wall)
    def _():
        height = h[...]
        for c in range(2):
            picked = v[c, LEVELS]
            for level in range(1, LEVELS):
                picked = jnp.where(height == level, v[c, level], picked)
            for r in range(group):
                j, off = (r * block) // LANES, (r * block) % LANES
                part = picked[:, j * LANES : (j + 1) * LANES]
                if off:
                    part = pltpu.roll(part, LANES - off, 1)
                stage[r, c] = part
        sample_height = height.astype(jnp.float32) + 0.5
        for r in range(group):
            j, off = (r * block) // LANES, (r * block) % LANES
            part = sample_height[:, j * LANES : (j + 1) * LANES]
            if off:
                part = pltpu.roll(part, LANES - off, 1)
            stage[r, 2] = part
        tops[gy] = stage[me]

    pl.semaphore_wait(barrier, 2 + group - 1)

    def top_send(d):
        r = lax.rem(me + d, group)
        return pltpu.make_async_remote_copy(
            src_ref=stage.at[r], dst_ref=tops.at[gy], send_sem=t_send.at[d], recv_sem=t_recv.at[gy],
            device_id=(gx, r // n_gz, r % n_gz), device_id_type=MESH,
        )

    @pl.when(at_wall)
    def _():
        for d in range(1, group):
            top_send(d).start()

    def x_copies(k):
        depth = layers // CHUNKS
        zs = pl.ds((CHUNKS - 1 - k) * depth, depth)
        to_right = pltpu.make_async_remote_copy(
            src_ref=v_hbm.at[:, zs, pl.ds(rows - 1, 1)], dst_ref=xlo.at[:, zs],
            send_sem=x_send.at[2 * k], recv_sem=x_recv.at[2 * k],
            device_id=(right, gy, gz), device_id_type=MESH,
        )
        to_left = pltpu.make_async_remote_copy(
            src_ref=v_hbm.at[:, zs, pl.ds(0, 1)], dst_ref=xhi.at[:, zs],
            send_sem=x_send.at[2 * k + 1], recv_sem=x_recv.at[2 * k + 1],
            device_id=(left, gy, gz), device_id_type=MESH,
        )
        return to_right, to_left

    for k in range(CHUNKS):
        for copy in x_copies(k):
            copy.start()

    edge = (layers - 1) * (1 - gz)
    z_copy = pltpu.make_async_remote_copy(
        src_ref=v_hbm.at[:, edge], dst_ref=zhalo, send_sem=z_send.at[0], recv_sem=z_recv.at[0],
        device_id=(gx, gy, 1 - gz), device_id_type=MESH,
    )
    z_copy.start()

    loads[2].wait()
    loads[3].wait()
    lane = lax.broadcasted_iota(jnp.int32, (rows, LANES), 1)

    def pack(k, carry):
        low, high = carry
        c, z = k // layers, k % layers
        low = jnp.where(lane == k, pltpu.roll(v[c, z, :, :LANES], k, 1), low)
        high = jnp.where(lane == k, pltpu.roll(v[c, z, :, width - LANES :], k + 1, 1), high)
        return low, high

    zeros = jnp.zeros((rows, LANES), jnp.float32)
    low, high = lax.fori_loop(0, 3 * layers, pack, (zeros, zeros), unroll=4)
    ypack_lo[...] = low
    ypack_hi[...] = high
    y_copies = [
        pltpu.make_async_remote_copy(
            src_ref=ypack_hi, dst_ref=ylo, send_sem=y_send.at[0], recv_sem=y_recv.at[0],
            device_id=(gx, above, gz), device_id_type=MESH,
        ),
        pltpu.make_async_remote_copy(
            src_ref=ypack_lo, dst_ref=yhi, send_sem=y_send.at[1], recv_sem=y_recv.at[1],
            device_id=(gx, below, gz), device_id_type=MESH,
        ),
    ]
    for copy in y_copies:
        copy.start()

    loads[4].wait()

    def shear(i, carry):
        du = s[0, i + 1] - s[0, i]
        dv = s[1, i + 1] - s[1, i]
        eddy[i] = tab_ref[1, i] * jnp.sqrt(du * du + dv * dv + 1e-06)
        return carry

    lax.fori_loop(0, points - 1, shear, 0, unroll=3)

    def top_wait(src):
        pltpu.make_async_remote_copy(
            src_ref=stage.at[0], dst_ref=tops.at[src], send_sem=t_send.at[0], recv_sem=t_recv.at[src],
            device_id=(gx, gy, 1 - gz), device_id_type=MESH,
        ).wait_recv()

    for src in range(n_gy):

        @pl.when(me != src * n_gz)
        def _():
            top_wait(src)

    lane_wide = lax.broadcasted_iota(jnp.int32, (rows, cols), 1)
    halves = cols // LANES

    def interleave(field):
        parts = []
        for half in range(halves):
            source = (lane + half * LANES) // n_gy
            owner = (lane + half * LANES) % n_gy
            out = None
            for src in range(n_gy):
                got = jnp.take_along_axis(tops[src, field], source, axis=1, mode="promise_in_bounds")
                out = got if out is None else jnp.where(owner == src, got, out)
            parts.append(out)
        return jnp.concatenate(parts, axis=1)

    top_u, top_v, height = interleave(0), interleave(1), interleave(2)
    inv_height = 1.0 / height

    last = points - 1
    fresh_ref[0, last] = top_u
    fresh_ref[1, last] = top_v
    fresh_ref[0, 0] = jnp.zeros_like(top_u)
    fresh_ref[1, 0] = jnp.zeros_like(top_u)

    def eliminate(k, carry):
        share, cond, f_u, f_v = carry
        i = last - 1 - k
        cond_low = tab_ref[0, i - 1] * inv_height + eddy[i - 1]
        volume = tab_ref[2, i] * height
        held = volume + share
        inverse = 1.0 / (held + cond_low)
        f_u = (volume * s[0, i] + cond * f_u) * inverse
        f_v = (volume * s[1, i] + cond * f_v) * inverse
        coef_e[i] = cond_low * inverse
        coef_f[0, i] = f_u
        coef_f[1, i] = f_v
        return cond_low * (held * inverse), cond_low, f_u, f_v

    cond_top = tab_ref[0, last - 1] * inv_height + eddy[last - 1]
    _, cond, f_u, f_v = lax.fori_loop(0, points - 2, eliminate, (cond_top, cond_top, top_u, top_v), unroll=2)
    stress = (cond * f_u, cond * f_v)

    for src in range(n_gy):
        index = lane * n_gy + src
        index = jnp.where(index < cols, index, 0)
        for c in range(2):
            out = None
            for half in range(halves):
                got = jnp.take_along_axis(
                    stress[c][:, half * LANES : (half + 1) * LANES], index % LANES, axis=1, mode="promise_in_bounds"
                )
                out = got if out is None else jnp.where(index // LANES == half, got, out)
            back[src, c] = out

    def wall_send(src):
        return pltpu.make_async_remote_copy(
            src_ref=back.at[src], dst_ref=walls.at[me], send_sem=w_send.at[src], recv_sem=w_recv.at[me],
            device_id=(gx, src, 0), device_id_type=MESH,
        )

    for src in range(n_gy):

        @pl.when(me != src * n_gz)
        def _():
            wall_send(src).start()

    @pl.when(at_wall)
    def _():
        walls[me] = back[gy]

    def substitute(k, carry):
        u, w = carry
        i = k + 1
        e = coef_e[i]
        u = e * u + coef_f[0, i]
        w = e * w + coef_f[1, i]
        fresh_ref[0, i] = u
        fresh_ref[1, i] = w
        return u, w

    zero = jnp.zeros_like(top_u)
    lax.fori_loop(0, points - 2, substitute, (zero, zero), unroll=2)

    for copy in y_copies:
        copy.wait_recv()
    z_copy.wait_recv()
    loads[5].wait()

    disks = mask[0]
    for k in range(1, 8):
        disks = jnp.maximum(disks, mask[k])
    force = jnp.zeros((rows, width), jnp.float32)
    for k in range(8):
        force = force + jnp.where(disks == k + 1, thrust_ref[k], 0.0)
    plane[...] = force * time_step

    row = lax.broadcasted_iota(jnp.int32, (rows, width), 0)
    col = lax.broadcasted_iota(jnp.int32, (rows, width), 1)

    def layer(z, below_v, above_v, wall):
        vel, xn, xp, yn, yp = [], [], [], [], []
        for c in range(3):
            here = v[c, z]
            vel.append(here)
            xp.append(jnp.where(row == 0, xlo[c, z], pltpu.roll(here, 1, 0)))
            xn.append(jnp.where(row == rows - 1, xhi[c, z], pltpu.roll(here, rows - 1, 0)))
            slot = c * layers + z
            low = pltpu.roll(ylo[...], LANES - slot, 1)
            high = pltpu.roll(yhi[...], LANES - 1 - slot, 1)
            low = jnp.concatenate([low] * tiles, axis=1)
            high = jnp.concatenate([high] * tiles, axis=1)
            yp.append(jnp.where(col == 0, low, pltpu.roll(here, 1, 1)))
            yn.append(jnp.where(col == width - 1, high, pltpu.roll(here, width - 1, 1)))
        zn, zp = above_v, below_v
        d_x = [xn[c] - xp[c] for c in range(3)]
        d_y = [yn[c] - yp[c] for c in range(3)]
        d_z = [zn[c] - zp[c] for c in range(3)]
        diag = d_x[0] * d_x[0] + d_y[1] * d_y[1] + d_z[2] * d_z[2]
        s_xy, s_xz, s_yz = d_y[0] + d_x[1], d_z[0] + d_x[2], d_z[1] + d_y[2]
        cross = s_xy * s_xy + s_xz * s_xz + s_yz * s_yz
        strain = jnp.sqrt(0.5 * diag + (0.25 * cross + 1e-06))
        viscous = time_step * viscosity + (time_step * smag_coeff) * strain
        for c in range(3):
            total = (xn[c] + xp[c]) + (yn[c] + yp[c]) + (zn[c] + zp[c])
            flux = (
                (xn[c] * xn[0] - xp[c] * xp[0]) + (yn[c] * yn[1] - yp[c] * yp[1]) + (zn[c] * zn[2] - zp[c] * zp[2])
            )
            lap = total - 6.0 * vel[c]
            if wall is not None and c < 2:
                lap = lap + wall[0] * vel[c]
            out = vel[c] + (viscous * lap - (0.5 * time_step) * flux)
            if wall is not None and c < 2:
                out = out - time_step * wall[1][c]
            adv_ref[c, z] = out

    def velocity_at(z):
        return [v[c, z] for c in range(3)]

    def x_wait(k):
        for copy in x_copies(k):
            copy.wait_recv()

    depth = layers // CHUNKS
    x_wait(0)
    bottom = at_wall.astype(jnp.float32)
    layer(layers - 1, velocity_at(layers - 2), [zhalo[c] * bottom for c in range(3)], None)

    def inner(z, carry):
        layer(z, velocity_at(z - 1), velocity_at(z + 1), None)
        return carry

    lax.fori_loop(layers - depth, layers - 1, inner, 0)
    for k in range(1, CHUNKS):
        x_wait(k)
        low = (CHUNKS - 1 - k) * depth
        lax.fori_loop(max(low, 1), low + depth, inner, 0)

    def wall_wait(r):
        pltpu.make_async_remote_copy(
            src_ref=back.at[0], dst_ref=walls.at[r], send_sem=w_send.at[0], recv_sem=w_recv.at[r],
            device_id=(gx, gy, 1 - gz), device_id_type=MESH,
        ).wait_recv()

    @pl.when(at_wall)
    def _():
        for r in range(group):

            @pl.when(me != r)
            def _():
                wall_wait(r)

        wall = []
        for c in range(2):
            parts = []
            for j in range(tiles):
                out = None
                for r in range(group):
                    if (r * block) // LANES == j:
                        off = (r * block) % LANES
                        got = walls[r, c]
                        if off:
                            got = pltpu.roll(got, off, 1)
                        out = got if out is None else jnp.where(lane >= off, got, out)
                parts.append(out)
            wall.append(jnp.concatenate(parts, axis=1))
        layer(0, [jnp.zeros((rows, width), jnp.float32)] * 3, velocity_at(1), (1.0, wall))

        for k in range(8):
            adv_ref[2, 2 + k] = adv_ref[2, 2 + k] - jnp.where(mask[k] != 0, plane[...], 0.0)

    @pl.when(jnp.logical_not(at_wall))
    def _():
        layer(0, [zhalo[c] for c in range(3)], velocity_at(1), None)

    @pl.when(at_wall)
    def _():
        for d in range(1, group):
            top_send(d).wait_send()

    for src in range(n_gy):

        @pl.when(me != src * n_gz)
        def _():
            wall_send(src).wait_send()

    for k in range(CHUNKS):
        for copy in x_copies(k):
            copy.wait_send()
    for copy in y_copies:
        copy.wait_send()
    z_copy.wait_send()


def local(n_gx, n_gy, n_gz, velocity, column_state, height_index, rotor_mask, thrust):
    _, layers, rows, width = velocity.shape
    _, points, _, cols = column_state.shape
    group = n_gy * n_gz
    table = jnp.asarray(np.asarray(column_constants(points), np.float32))
    any_spec = pl.BlockSpec(memory_space=pl.ANY)
    smem_spec = pl.BlockSpec(memory_space=pltpu.SMEM)
    vmem_spec = pl.BlockSpec(memory_space=pltpu.VMEM)
    f32 = jnp.float32
    dma = pltpu.SemaphoreType.DMA
    scratch = [
        pltpu.VMEM(velocity.shape, f32),
        pltpu.VMEM(column_state.shape, f32),
        pltpu.VMEM(height_index.shape, jnp.int32),
        pltpu.VMEM((8, rows, width), jnp.int32),
        pltpu.VMEM((points - 1, rows, cols), f32),
        pltpu.VMEM((points - 1, rows, cols), f32),
        pltpu.VMEM((2, points - 1, rows, cols), f32),
        pltpu.VMEM((3, layers, 1, width), f32),
        pltpu.VMEM((3, layers, 1, width), f32),
        pltpu.VMEM((3, rows, width), f32),
        pltpu.VMEM((rows, LANES), f32),
        pltpu.VMEM((rows, LANES), f32),
        pltpu.VMEM((rows, LANES), f32),
        pltpu.VMEM((rows, LANES), f32),
        pltpu.VMEM((group, 3, rows, LANES), f32),
        pltpu.VMEM((n_gy, 3, rows, LANES), f32),
        pltpu.VMEM((n_gy, 2, rows, LANES), f32),
        pltpu.VMEM((group, 2, rows, LANES), f32),
        pltpu.VMEM((rows, width), f32),
        dma((6,)),
        dma((2 * CHUNKS,)), dma((2 * CHUNKS,)),
        dma((2,)), dma((2,)),
        dma((1,)), dma((1,)),
        dma((group,)), dma((n_gy,)),
        dma((n_gy,)), dma((group,)),
    ]
    sizes = (n_gx, n_gy, n_gz, layers, rows, width, points, cols)
    return pl.pallas_call(
        functools.partial(kernel, sizes),
        out_shape=(
            jax.ShapeDtypeStruct(velocity.shape, f32),
            jax.ShapeDtypeStruct(column_state.shape, f32),
        ),
        in_specs=[any_spec] * 4 + [smem_spec] * 2,
        out_specs=(vmem_spec, vmem_spec),
        scratch_shapes=scratch,
        compiler_params=pltpu.CompilerParams(
            collective_id=0, has_side_effects=True, vmem_limit_bytes=32 * 1024 * 1024
        ),
    )(velocity, column_state, height_index, rotor_mask, thrust, table)


def solution(mesh):
    in_specs = (
        P(None, "gz", "gx", "gy"),
        P(None, None, "gx", ("gy", "gz")),
        P("gx", "gy"),
        P("gz", "gx", "gy"),
        P(),
    )
    out_specs = (P(None, "gz", "gx", "gy"), P(None, None, "gx", ("gy", "gz")))
    run = functools.partial(local, mesh.shape["gx"], mesh.shape["gy"], mesh.shape["gz"])
    return jax.shard_map(run, mesh=mesh, in_specs=in_specs, out_specs=out_specs, check_vma=False)
```

time: 166 us -> 22.2 us (0.13)
  local copies, waits for them, and re-layouts: 80.5 us -> 7.2 us
  waiting for transfers between devices: 39.5 us -> 0 us
  other arithmetic: 24.3 us -> 0 us
  starting transfers between devices: 18.8 us -> 0 us
  Pallas kernels: 0 us -> 14 us
    ppermute x6 -> x0, waiting for transfers between devices: 27.9 us -> none  [the longest x3 19.5 us: with_halo(): lax.ppermute(lax.slice_in_dim(block, 0, width, axis=dim), axis, backward)]
    unnamed x58 -> x14, local copies, waits for them, and re-layouts: 32.9 us -> 7.2 us
    reshape x3 -> x0, local copies, waits for them, and re-layouts: 25.7 us -> none  [the longest x1 12.2 us: lower(): columns_in.reshape(-1, block_len, span_count)]
    pallas_call x0 -> x1, Pallas kernels: none -> 14 us  [local(): pl.pallas_call(functools.partial(kernel, sizes), out_shape=(jax.ShapeDtyp...]
    all_to_all x2 -> x0, waiting for transfers between devices: 11.6 us -> none  [the longest x1 11.6 us: lift(): lax.all_to_all(flat, ('gy', 'gz'), split_axis=1, concat_axis=1, tiled=True)]
    ppermute x6 -> x0, starting transfers between devices: 11.1 us -> none  [the longest x3 8.51 us: with_halo(): lax.ppermute(lax.slice_in_dim(block, 0, width, axis=dim), axis, backward)]
    all_to_all x2 -> x0, starting transfers between devices: 7.75 us -> none  [the longest x1 3.92 us: lower(): lax.all_to_all(slots.reshape(-1, width_ground), ('gy', 'gz'), split_axis=...]
    all_to_all x3 -> x0, local copies, waits for them, and re-layouts: 7.47 us -> none  [the longest x2 4.79 us: lift(): lax.all_to_all(flat, ('gy', 'gz'), split_axis=1, concat_axis=1, tiled=True)]
  transfers between devices with their start and end apart: 8 -> 0, of which waited for: 3 -> 0; matrix products, arithmetic and copies ran while one was open for 37% -> 0% of each run, Pallas kernels for 0% -> 0%
where the time goes in v1:
time: 22.2 us; the launch traced here: 21.8 us
  Pallas kernels  14 us (63%)
  local copies, waits for them, and re-layouts  7.2 us (32%)
  between operations  0.65 us (3%)
    pallas_call x1, Pallas kernels, local(): pl.pallas_call(functools.partial(kernel, sizes), out_shape=(jax.ShapeDtyp...  14 us
    unnamed x14, local copies, waits for them, and re-layouts  7.2 us

profile of v1, /device:TPU:0, one launch (start us, length us, event | category | flops | bytes accessed | tf_op | source)
XLA Modules:
  0.0 21.8 jit_solution(6165846112532933761)
XLA Ops:
  0.6 0.0 copy-start
  0.6 1.2 %copy-done = f32[2,64,8,256]{3,2,1,0:T(8,128)S(1)} copy-done((f32[2,64,8,256]{3,2,1,0:T(8,128)S(1)}, f32[2,64,8,256]{3,2,1,0:T(8,128)}, u32[]{:S(2)}) %copy-start) | copy-done | bytes 1048600
  1.9 0.0 copy-start.1
  1.9 1.1 %copy-done.1 = f32[3,16,8,512]{3,2,1,0:T(8,128)S(1)} copy-done((f32[3,16,8,512]{3,2,1,0:T(8,128)S(1)}, f32[3,16,8,512]{3,2,1,0:T(8,128)}, u32[]{:S(2)}) %copy-start.1) | copy-done | bytes 786456
  3.0 0.0 copy-start.2
  3.0 0.9 %copy-done.2 = s32[16,8,512]{2,1,0:T(8,128)S(1)} copy-done((s32[16,8,512]{2,1,0:T(8,128)S(1)}, s32[16,8,512]{2,1,0:T(8,128)}, u32[]{:S(2)}) %copy-start.2) | copy-done | bytes 262168
  3.9 0.0 copy-start.3
  3.9 0.7 %copy-done.3 = s32[8,512]{1,0:T(8,128)S(1)} copy-done((s32[8,512]{1,0:T(8,128)S(1)}, s32[8,512]{1,0:T(8,128)}, u32[]{:S(2)}) %copy-start.3) | copy-done | bytes 16408
  4.7 0.0 copy-start.4
  4.7 0.7 %copy-done.4 = f32[3,63]{1,0:T(4,128)S(1)} copy-done((f32[3,63]{1,0:T(4,128)S(1)}, f32[3,63]{1,0:T(4,128)}, u32[]{:S(2)}) %copy-start.4) | copy-done | bytes 780
  5.3 0.0 copy-start.5
  5.3 0.7 %copy-done.5 = f32[8]{0:T(128)S(1)} copy-done((f32[8]{0:T(128)S(1)}, f32[8]{0:T(128)}, u32[]{:S(2)}) %copy-start.5) | copy-done | bytes 56
  6.0 14.0 %shard_map.77 = (f32[3,16,8,512]{3,2,1,0:T(8,128)S(1)}, f32[2,64,8,256]{3,2,1,0:T(8,128)S(1)}) custom-call(f32[3,16,8,512]{3,2,1,0:T(8,128)S(1)} %copy-done.1, f32[2,64,8,256]{3,2,1,0:T(8,128)S(1)} %copy-done, s32[8,512]{1,0:T(8,128)S(1)} %copy-done.3, s32[16,8,512]{2,1,0:T(8,128)S(1)} %copy-done.2, f32[8]{0:T(128)S(1)} %copy-done.5, f32[3,63]{1,0:T(4,128)S(1)} %copy-done.4), custom_call_target="tpu_custom_call" | custom-call | tf_op jit(solution)/shard_map/pallas_call | solution.py:446
  20.0 0.9 %copy.10 = f32[3,16,8,512]{3,2,1,0:T(8,128)} copy(f32[3,16,8,512]{3,2,1,0:T(8,128)S(1)} %get-tuple-element.4) | data formatting | bytes 1572864
  20.9 1.0 %copy.11 = f32[2,64,8,256]{3,2,1,0:T(8,128)} copy(f32[2,64,8,256]{3,2,1,0:T(8,128)S(1)} %get-tuple-element.5) | data formatting | bytes 2097152
Async XLA Ops:
  0.6 1.2 %copy-start = (f32[2,64,8,256]{3,2,1,0:T(8,128)S(1)}, f32[2,64,8,256]{3,2,1,0:T(8,128)}, u32[]{:S(2)}) copy-start(f32[2,64,8,256]{3,2,1,0:T(8,128)} %s_hbm.1) | copy-start | bytes 3145732
  1.9 1.1 %copy-start.1 = (f32[3,16,8,512]{3,2,1,0:T(8,128)S(1)}, f32[3,16,8,512]{3,2,1,0:T(8,128)}, u32[]{:S(2)}) copy-start(f32[3,16,8,512]{3,2,1,0:T(8,128)} %v_hbm.1) | copy-start | bytes 2359300
  3.0 0.9 %copy-start.2 = (s32[16,8,512]{2,1,0:T(8,128)S(1)}, s32[16,8,512]{2,1,0:T(8,128)}, u32[]{:S(2)}) copy-start(s32[16,8,512]{2,1,0:T(8,128)} %m_hbm.1) | copy-start | bytes 786436
  3.9 0.7 %copy-start.3 = (s32[8,512]{1,0:T(8,128)S(1)}, s32[8,512]{1,0:T(8,128)}, u32[]{:S(2)}) copy-start(s32[8,512]{1,0:T(8,128)} %h_hbm.1) | copy-start | bytes 49156
  4.7 0.7 %copy-start.4 = (f32[3,63]{1,0:T(4,128)S(1)}, f32[3,63]{1,0:T(4,128)}, u32[]{:S(2)}) copy-start(f32[3,63]{1,0:T(4,128)} %constant.2.clone.tab_ref) | copy-start | bytes 2272
  5.3 0.7 %copy-start.5 = (f32[8]{0:T(128)S(1)}, f32[8]{0:T(128)}, u32[]{:S(2)}) copy-start(f32[8]{0:T(128)} %thrust_ref.1) | copy-start | bytes 100

commit v2 on v1

--- a/solution.py
+++ b/solution.py
@@ -36,9 +36,9 @@
 
 def kernel(
     sizes,
-    v_hbm, s_hbm, h_hbm, m_hbm, thrust_ref, tab_ref,
+    v_hbm, s_hbm, h_hbm, m_hbm, t_hbm,
     adv_ref, fresh_ref,
-    v, s, h, mask, eddy, coef_e, coef_f,
+    v, s, h, mask, thrust_ref, tab_ref, eddy, coef_e, coef_f,
     xlo, xhi, zhalo, ypack_lo, ypack_hi, ylo, yhi,
     stage, tops, back, walls, plane,
     load_sem, x_send, x_recv, y_send, y_recv, z_send, z_recv, t_send, t_recv, w_send, w_recv,
@@ -66,6 +66,7 @@
         pltpu.make_async_copy(v_hbm.at[2], v.at[2], load_sem.at[3]),
         pltpu.make_async_copy(s_hbm, s, load_sem.at[4]),
         pltpu.make_async_copy(m_hbm.at[pl.ds(2, 8)], mask, load_sem.at[5]),
+        pltpu.make_async_copy(t_hbm, thrust_ref, load_sem.at[6]),
     ]
     for load in loads:
         load.start()
@@ -76,6 +77,10 @@
     for d in range(1, group):
         r = lax.rem(me + d, group)
         pl.semaphore_signal(barrier, inc=1, device_id=(gx, r // n_gz, r % n_gz), device_id_type=MESH)
+
+    for j, entries in enumerate(column_constants(points)):
+        for i, entry in enumerate(entries):
+            tab_ref[j, i] = entry
 
     loads[0].wait()
     loads[1].wait()
@@ -279,6 +284,7 @@
         copy.wait_recv()
     z_copy.wait_recv()
     loads[5].wait()
+    loads[6].wait()
 
     disks = mask[0]
     for k in range(1, 8):
@@ -409,9 +415,7 @@
     _, layers, rows, width = velocity.shape
     _, points, _, cols = column_state.shape
     group = n_gy * n_gz
-    table = jnp.asarray(np.asarray(column_constants(points), np.float32))
-    any_spec = pl.BlockSpec(memory_space=pl.ANY)
-    smem_spec = pl.BlockSpec(memory_space=pltpu.SMEM)
+    hbm_spec = pl.BlockSpec(memory_space=pltpu.HBM)
     vmem_spec = pl.BlockSpec(memory_space=pltpu.VMEM)
     f32 = jnp.float32
     dma = pltpu.SemaphoreType.DMA
@@ -420,6 +424,8 @@
         pltpu.VMEM(column_state.shape, f32),
         pltpu.VMEM(height_index.shape, jnp.int32),
         pltpu.VMEM((8, rows, width), jnp.int32),
+        pltpu.SMEM(thrust.shape, f32),
+        pltpu.SMEM((3, points - 1), f32),
         pltpu.VMEM((points - 1, rows, cols), f32),
         pltpu.VMEM((points - 1, rows, cols), f32),
         pltpu.VMEM((2, points - 1, rows, cols), f32),
@@ -435,7 +441,7 @@
         pltpu.VMEM((n_gy, 2, rows, LANES), f32),
         pltpu.VMEM((group, 2, rows, LANES), f32),
         pltpu.VMEM((rows, width), f32),
-        dma((6,)),
+        dma((7,)),
         dma((2 * CHUNKS,)), dma((2 * CHUNKS,)),
         dma((2,)), dma((2,)),
         dma((1,)), dma((1,)),
@@ -449,13 +455,13 @@
             jax.ShapeDtypeStruct(velocity.shape, f32),
             jax.ShapeDtypeStruct(column_state.shape, f32),
         ),
-        in_specs=[any_spec] * 4 + [smem_spec] * 2,
+        in_specs=[hbm_spec] * 5,
         out_specs=(vmem_spec, vmem_spec),
         scratch_shapes=scratch,
         compiler_params=pltpu.CompilerParams(
             collective_id=0, has_side_effects=True, vmem_limit_bytes=32 * 1024 * 1024
         ),
-    )(velocity, column_state, height_index, rotor_mask, thrust, table)
+    )(*[pltpu.with_memory_space_constraint(a, pltpu.HBM) for a in (velocity, column_state, height_index, rotor_mask, thrust)])
 
 
 def solution(mesh):

time: 22.2 us -> 15.7 us (0.71)
  local copies, waits for them, and re-layouts: 7.2 us -> 1.85 us
  Pallas kernels: 14 us -> 13 us
    unnamed x14 -> x2, local copies, waits for them, and re-layouts: 7.2 us -> 1.85 us
    pallas_call x1, Pallas kernels: 14 us -> 13 us  [local(): pl.pallas_call(functools.partial(kernel, sizes), out_shape=(jax.ShapeDtyp...]
where the time goes in v2:
time: 15.7 us; the launch traced here: 15.5 us
  Pallas kernels  13 us (83%)
  local copies, waits for them, and re-layouts  1.85 us (12%)
  between operations  0.64 us (4%)
    pallas_call x1, Pallas kernels, local(): pl.pallas_call(functools.partial(kernel, sizes), out_shape=(jax.ShapeDtyp...  13 us
    unnamed x2, local copies, waits for them, and re-layouts  1.85 us

profile of v2, /device:TPU:0, one launch (start us, length us, event | category | flops | bytes accessed | tf_op | source)
XLA Modules:
  0.0 15.5 jit_solution(6790514981498247548)
XLA Ops:
  0.6 13.0 %shard_map.68 = (f32[3,16,8,512]{3,2,1,0:T(8,128)S(1)}, f32[2,64,8,256]{3,2,1,0:T(8,128)S(1)}) custom-call(f32[3,16,8,512]{3,2,1,0:T(8,128)} %v_hbm.1, f32[2,64,8,256]{3,2,1,0:T(8,128)} %s_hbm.1, s32[8,512]{1,0:T(8,128)} %h_hbm.1, s32[16,8,512]{2,1,0:T(8,128)} %m_hbm.1, f32[8]{0:T(128)} %t_hbm.1), custom_call_target="tpu_custom_call" | custom-call | tf_op jit(solution)/shard_map/pallas_call | solution.py:452
  13.6 0.9 %copy.9 = f32[3,16,8,512]{3,2,1,0:T(8,128)} copy(f32[3,16,8,512]{3,2,1,0:T(8,128)S(1)} %get-tuple-element.4) | data formatting | bytes 1572864
  14.5 1.0 %copy.10 = f32[2,64,8,256]{3,2,1,0:T(8,128)} copy(f32[2,64,8,256]{3,2,1,0:T(8,128)S(1)} %get-tuple-element.5) | data formatting | bytes 2097152

commit v3 on v2

--- a/solution.py
+++ b/solution.py
@@ -41,7 +41,7 @@
     v, s, h, mask, thrust_ref, tab_ref, eddy, coef_e, coef_f,
     xlo, xhi, zhalo, ypack_lo, ypack_hi, ylo, yhi,
     stage, tops, back, walls, plane,
-    load_sem, x_send, x_recv, y_send, y_recv, z_send, z_recv, t_send, t_recv, w_send, w_recv,
+    load_sem, x_send, x_recv, y_send, y_recv, z_send, z_recv, t_send, t_recv, w_send, w_recv, ready,
 ):
     n_gx, n_gy, n_gz, layers, rows, width, points, cols = sizes
     group = n_gy * n_gz
@@ -73,7 +73,11 @@
 
     barrier = pltpu.get_barrier_semaphore()
     for side in (left, right):
-        pl.semaphore_signal(barrier, inc=1, device_id=(side, gy, gz), device_id_type=MESH)
+
+        @pl.when(side != 0)
+        def _():
+            pl.semaphore_signal(barrier, inc=1, device_id=(side, gy, gz), device_id_type=MESH)
+
     for d in range(1, group):
         r = lax.rem(me + d, group)
         pl.semaphore_signal(barrier, inc=1, device_id=(gx, r // n_gz, r % n_gz), device_id_type=MESH)
@@ -107,7 +111,21 @@
             stage[r, 2] = part
         tops[gy] = stage[me]
 
-    pl.semaphore_wait(barrier, 2 + group - 1)
+    first = gx == 0
+
+    @pl.when(first)
+    def _():
+        pl.semaphore_wait(barrier, group - 1)
+
+    @pl.when(jnp.logical_not(first))
+    def _():
+        pl.semaphore_wait(barrier, 2 + group - 1)
+        for side in (left, right):
+
+            @pl.when(side == 0)
+            def _():
+                pl.semaphore_signal(ready, inc=1, device_id=(side, gy, gz), device_id_type=MESH)
+
 
     def top_send(d):
         r = lax.rem(me + d, group)
@@ -136,9 +154,11 @@
         )
         return to_right, to_left
 
-    for k in range(CHUNKS):
-        for copy in x_copies(k):
-            copy.start()
+    @pl.when(jnp.logical_not(first))
+    def _():
+        for k in range(CHUNKS):
+            for copy in x_copies(k):
+                copy.start()
 
     edge = (layers - 1) * (1 - gz)
     z_copy = pltpu.make_async_remote_copy(
@@ -266,6 +286,13 @@
     @pl.when(at_wall)
     def _():
         walls[me] = back[gy]
+
+    @pl.when(first)
+    def _():
+        pl.semaphore_wait(ready, 2)
+        for k in range(CHUNKS):
+            for copy in x_copies(k):
+                copy.start()
 
     def substitute(k, carry):
         u, w = carry
@@ -349,7 +376,7 @@
         layer(z, velocity_at(z - 1), velocity_at(z + 1), None)
         return carry
 
-    lax.fori_loop(layers - depth, layers - 1, inner, 0)
+    lax.fori_loop(max(layers - depth, 1), layers - 1, inner, 0)
     for k in range(1, CHUNKS):
         x_wait(k)
         low = (CHUNKS - 1 - k) * depth
@@ -409,6 +436,15 @@
     for copy in y_copies:
         copy.wait_send()
     z_copy.wait_send()
+
+
+def write_out(advanced, fresh, advanced_hbm, fresh_hbm, sem):
+    copies = [pltpu.make_async_copy(fresh.at[c], fresh_hbm.at[c], sem.at[c]) for c in range(2)]
+    copies += [pltpu.make_async_copy(advanced.at[c], advanced_hbm.at[c], sem.at[2 + c]) for c in range(3)]
+    for copy in copies:
+        copy.start()
+    for copy in copies:
+        copy.wait()
 
 
 def local(n_gx, n_gy, n_gz, velocity, column_state, height_index, rotor_mask, thrust):
@@ -447,9 +483,10 @@
         dma((1,)), dma((1,)),
         dma((group,)), dma((n_gy,)),
         dma((n_gy,)), dma((group,)),
+        pltpu.SemaphoreType.REGULAR,
     ]
     sizes = (n_gx, n_gy, n_gz, layers, rows, width, points, cols)
-    return pl.pallas_call(
+    advanced, fresh = pl.pallas_call(
         functools.partial(kernel, sizes),
         out_shape=(
             jax.ShapeDtypeStruct(velocity.shape, f32),
@@ -462,6 +499,21 @@
             collective_id=0, has_side_effects=True, vmem_limit_bytes=32 * 1024 * 1024
         ),
     )(*[pltpu.with_memory_space_constraint(a, pltpu.HBM) for a in (velocity, column_state, height_index, rotor_mask, thrust)])
+
+    return pl.pallas_call(
+        write_out,
+        out_shape=(
+            jax.ShapeDtypeStruct(velocity.shape, f32),
+            jax.ShapeDtypeStruct(column_state.shape, f32),
+        ),
+        in_specs=(vmem_spec, vmem_spec),
+        out_specs=(hbm_spec, hbm_spec),
+        scratch_shapes=[dma((5,))],
+        compiler_params=pltpu.CompilerParams(vmem_limit_bytes=8 * 1024 * 1024),
+    )(
+        pltpu.with_memory_space_constraint(advanced, pltpu.VMEM),
+        pltpu.with_memory_space_constraint(fresh, pltpu.VMEM),
+    )
 
 
 def solution(mesh):

time: 15.7 us -> 14.4 us (0.917)
  local copies, waits for them, and re-layouts: 1.85 us -> 0 us
  Pallas kernels: 13 us -> 13.6 us
    unnamed x2 -> x0, local copies, waits for them, and re-layouts: 1.85 us -> none
    pallas_call x0 -> x1, Pallas kernels: none -> 1.27 us  [local(): pl.pallas_call(write_out, out_shape=(jax.ShapeDtypeStruct(velocity.shape,...]
    pallas_call x1, Pallas kernels: 13 us -> 12.3 us  [local(): pl.pallas_call(functools.partial(kernel, sizes), out_shape=(jax.ShapeDtyp...]
where the time goes in v3:
time: 14.4 us; the launch traced here: 14.2 us
  Pallas kernels  13.6 us (94%)
  between operations  0.64 us (4%)
    pallas_call x1, Pallas kernels, local(): pl.pallas_call(functools.partial(kernel, sizes), out_shape=(jax.ShapeDtyp...  12.3 us
    pallas_call x1, Pallas kernels, local(): pl.pallas_call(write_out, out_shape=(jax.ShapeDtypeStruct(velocity.shape,...  1.27 us

profile of v3, /device:TPU:0, one launch (start us, length us, event | category | flops | bytes accessed | tf_op | source)
XLA Modules:
  0.0 14.2 jit_solution(1192379532481809545)
XLA Ops:
  0.6 12.3 %shard_map.68 = (f32[3,16,8,512]{3,2,1,0:T(8,128)S(1)}, f32[2,64,8,256]{3,2,1,0:T(8,128)S(1)}) custom-call(f32[3,16,8,512]{3,2,1,0:T(8,128)} %v_hbm.1, f32[2,64,8,256]{3,2,1,0:T(8,128)} %s_hbm.1, s32[8,512]{1,0:T(8,128)} %h_hbm.1, s32[16,8,512]{2,1,0:T(8,128)} %m_hbm.1, f32[8]{0:T(128)} %t_hbm.1), custom_call_target="tpu_custom_call" | custom-call | tf_op jit(solution)/shard_map/pallas_call | solution.py:489
  12.9 1.3 %shard_map.69 = (f32[3,16,8,512]{3,2,1,0:T(8,128)}, f32[2,64,8,256]{3,2,1,0:T(8,128)}) custom-call(f32[3,16,8,512]{3,2,1,0:T(8,128)S(1)} %get-tuple-element.4.advanced, f32[2,64,8,256]{3,2,1,0:T(8,128)S(1)} %get-tuple-element.5.fresh), custom_call_target="tpu_custom_call" | custom-call | tf_op jit(solution)/shard_map/pallas_call | solution.py:503

commit v4 on v3

--- a/solution.py
+++ b/solution.py
@@ -40,7 +40,7 @@
     adv_ref, fresh_ref,
     v, s, h, mask, thrust_ref, tab_ref, eddy, coef_e, coef_f,
     xlo, xhi, zhalo, ypack_lo, ypack_hi, ylo, yhi,
-    stage, tops, back, walls, plane,
+    stage, tops, back, walls, push,
     load_sem, x_send, x_recv, y_send, y_recv, z_send, z_recv, t_send, t_recv, w_send, w_recv, ready,
 ):
     n_gx, n_gy, n_gz, layers, rows, width, points, cols = sizes
@@ -71,16 +71,56 @@
     for load in loads:
         load.start()
 
+    first = gx == 0
+
+    def is_lead(x, y, z):
+        return (y == 0) & (z == 0) & ((x == 1) | (x == n_gx - 1))
+
+    lead = is_lead(gx, gy, gz)
+    plain = jnp.logical_not(first | lead)
+    mates = [(gx, r // n_gz, r % n_gz) for r in [lax.rem(me + d, group) for d in range(1, group)]]
     barrier = pltpu.get_barrier_semaphore()
+
+    def tell(semaphore, device):
+        pl.semaphore_signal(semaphore, inc=1, device_id=device, device_id_type=MESH)
+
     for side in (left, right):
 
-        @pl.when(side != 0)
+        @pl.when((side != 0) & (first | jnp.logical_not(is_lead(side, gy, gz))))
         def _():
-            pl.semaphore_signal(barrier, inc=1, device_id=(side, gy, gz), device_id_type=MESH)
-
-    for d in range(1, group):
-        r = lax.rem(me + d, group)
-        pl.semaphore_signal(barrier, inc=1, device_id=(gx, r // n_gz, r % n_gz), device_id_type=MESH)
+            tell(barrier, (side, gy, gz))
+
+    for mate in mates:
+
+        @pl.when(jnp.logical_not(is_lead(*mate)))
+        def _():
+            tell(barrier, mate)
+
+    def x_copies(k):
+        depth = layers // CHUNKS
+        zs = pl.ds((CHUNKS - 1 - k) * depth, depth)
+        to_right = pltpu.make_async_remote_copy(
+            src_ref=v_hbm.at[:, zs, pl.ds(rows - 1, 1)], dst_ref=xlo.at[:, zs],
+            send_sem=x_send.at[2 * k], recv_sem=x_recv.at[2 * k],
+            device_id=(right, gy, gz), device_id_type=MESH,
+        )
+        to_left = pltpu.make_async_remote_copy(
+            src_ref=v_hbm.at[:, zs, pl.ds(0, 1)], dst_ref=xhi.at[:, zs],
+            send_sem=x_send.at[2 * k + 1], recv_sem=x_recv.at[2 * k + 1],
+            device_id=(left, gy, gz), device_id_type=MESH,
+        )
+        return to_right, to_left
+
+    @pl.when(lead)
+    def _():
+        pl.semaphore_wait(barrier, 1)
+        for way, side in ((0, right), (1, left)):
+
+            @pl.when(side == 0)
+            def _():
+                tell(ready, (side, gy, gz))
+                for k in range(CHUNKS):
+                    x_copies(k)[way].start()
 
     for j, entries in enumerate(column_constants(points)):
         for i, entry in enumerate(entries):
@@ -111,21 +151,28 @@
             stage[r, 2] = part
         tops[gy] = stage[me]
 
-    first = gx == 0
-
     @pl.when(first)
     def _():
         pl.semaphore_wait(barrier, group - 1)
 
-    @pl.when(jnp.logical_not(first))
-    def _():
-        pl.semaphore_wait(barrier, 2 + group - 1)
+    @pl.when(lead)
+    def _():
+        pl.semaphore_wait(ready, group)
+
+    @pl.when(plain)
+    def _():
+        pl.semaphore_wait(barrier, group + 1)
         for side in (left, right):
 
-            @pl.when(side == 0)
+            @pl.when((side == 0) | is_lead(side, gy, gz))
             def _():
-                pl.semaphore_signal(ready, inc=1, device_id=(side, gy, gz), device_id_type=MESH)
-
+                tell(ready, (side, gy, gz))
+
+        for mate in mates:
+
+            @pl.when(is_lead(*mate))
+            def _():
+                tell(ready, mate)
 
     def top_send(d):
         r = lax.rem(me + d, group)
@@ -139,22 +186,16 @@
         for d in range(1, group):
             top_send(d).start()
 
-    def x_copies(k):
-        depth = layers // CHUNKS
-        zs = pl.ds((CHUNKS - 1 - k) * depth, depth)
-        to_right = pltpu.make_async_remote_copy(
-            src_ref=v_hbm.at[:, zs, pl.ds(rows - 1, 1)], dst_ref=xlo.at[:, zs],
-            send_sem=x_send.at[2 * k], recv_sem=x_recv.at[2 * k],
-            device_id=(right, gy, gz), device_id_type=MESH,
-        )
-        to_left = pltpu.make_async_remote_copy(
-            src_ref=v_hbm.at[:, zs, pl.ds(0, 1)], dst_ref=xhi.at[:, zs],
-            send_sem=x_send.at[2 * k + 1], recv_sem=x_recv.at[2 * k + 1],
-            device_id=(left, gy, gz), device_id_type=MESH,
-        )
-        return to_right, to_left
-
-    @pl.when(jnp.logical_not(first))
+    @pl.when(lead)
+    def _():
+        for way, side in ((0, right), (1, left)):
+
+            @pl.when(side != 0)
+            def _():
+                for k in range(CHUNKS):
+                    x_copies(k)[way].start()
+
+    @pl.when(plain)
     def _():
         for k in range(CHUNKS):
             for copy in x_copies(k):
@@ -319,7 +360,12 @@
     force = jnp.zeros((rows, width), jnp.float32)
     for k in range(8):
         force = force + jnp.where(disks == k + 1, thrust_ref[k], 0.0)
-    plane[...] = force * time_step
+    force = force * time_step
+    for z in range(layers):
+        if 2 <= z < 10:
+            push[z] = jnp.where(jnp.logical_and(mask[z - 2] != 0, at_wall), force, 0.0)
+        else:
+            push[z] = jnp.zeros_like(force)
 
     row = lax.broadcasted_iota(jnp.int32, (rows, width), 0)
     col = lax.broadcasted_iota(jnp.int32, (rows, width), 1)
@@ -358,6 +404,8 @@
             out = vel[c] + (viscous * lap - (0.5 * time_step) * flux)
             if wall is not None and c < 2:
                 out = out - time_step * wall[1][c]
+            if c == 2:
+                out = out - push[z]
             adv_ref[c, z] = out
 
     def velocity_at(z):
@@ -411,9 +459,6 @@
                 parts.append(out)
             wall.append(jnp.concatenate(parts, axis=1))
         layer(0, [jnp.zeros((rows, width), jnp.float32)] * 3, velocity_at(1), (1.0, wall))
-
-        for k in range(8):
-            adv_ref[2, 2 + k] = adv_ref[2, 2 + k] - jnp.where(mask[k] != 0, plane[...], 0.0)
 
     @pl.when(jnp.logical_not(at_wall))
     def _():
@@ -476,7 +521,7 @@
         pltpu.VMEM((n_gy, 3, rows, LANES), f32),
         pltpu.VMEM((n_gy, 2, rows, LANES), f32),
         pltpu.VMEM((group, 2, rows, LANES), f32),
-        pltpu.VMEM((rows, width), f32),
+        pltpu.VMEM((layers, rows, width), f32),
         dma((7,)),
         dma((2 * CHUNKS,)), dma((2 * CHUNKS,)),
         dma((2,)), dma((2,)),

time: 14.4 us -> 13.4 us (0.931)
  the two profiles are of different devices: /device:TPU:0 before, /device:TPU:1 now
where the time goes in v4:
time: 13.4 us; the launch traced here: 13.1 us
  Pallas kernels  12.5 us (93%)
  between operations  0.64 us (5%)
    pallas_call x1, Pallas kernels, local(): pl.pallas_call(functools.partial(kernel, sizes), out_shape=(jax.ShapeDtyp...  11.2 us
    pallas_call x1, Pallas kernels, local(): pl.pallas_call(write_out, out_shape=(jax.ShapeDtypeStruct(velocity.shape,...  1.27 us

profile of v4, /device:TPU:1, one launch (start us, length us, event | category | flops | bytes accessed | tf_op | source)
XLA Modules:
  0.0 13.1 jit_solution(11258836009125412248)
XLA Ops:
  0.6 11.2 %shard_map.68 = (f32[3,16,8,512]{3,2,1,0:T(8,128)S(1)}, f32[2,64,8,256]{3,2,1,0:T(8,128)S(1)}) custom-call(f32[3,16,8,512]{3,2,1,0:T(8,128)} %v_hbm.1, f32[2,64,8,256]{3,2,1,0:T(8,128)} %s_hbm.1, s32[8,512]{1,0:T(8,128)} %h_hbm.1, s32[16,8,512]{2,1,0:T(8,128)} %m_hbm.1, f32[8]{0:T(128)} %t_hbm.1), custom_call_target="tpu_custom_call" | custom-call | tf_op jit(solution)/shard_map/pallas_call | solution.py:534
  11.9 1.3 %shard_map.69 = (f32[3,16,8,512]{3,2,1,0:T(8,128)}, f32[2,64,8,256]{3,2,1,0:T(8,128)}) custom-call(f32[3,16,8,512]{3,2,1,0:T(8,128)S(1)} %get-tuple-element.4.advanced, f32[2,64,8,256]{3,2,1,0:T(8,128)S(1)} %get-tuple-element.5.fresh), custom_call_target="tpu_custom_call" | custom-call | tf_op jit(solution)/shard_map/pallas_call | solution.py:548

commit v5 on v4

--- a/solution.py
+++ b/solution.py
@@ -74,7 +74,7 @@
     first = gx == 0
 
     def is_lead(x, y, z):
-        return (y == 0) & (z == 0) & ((x == 1) | (x == n_gx - 1))
+        return (y == 0) & ((x == 1) | (x == n_gx - 1))
 
     lead = is_lead(gx, gy, gz)
     plain = jnp.logical_not(first | lead)
@@ -157,7 +157,7 @@
 
     @pl.when(lead)
     def _():
-        pl.semaphore_wait(ready, group)
+        pl.semaphore_wait(ready, group - n_gz + 1)
 
     @pl.when(plain)
     def _():
@@ -258,7 +258,15 @@
         def _():
             top_wait(src)
 
-    lane_wide = lax.broadcasted_iota(jnp.int32, (rows, cols), 1)
+    def answer(now):
+        @pl.when(first & now)
+        def _():
+            pl.semaphore_wait(ready, 2)
+            for k in range(CHUNKS):
+                for copy in x_copies(k):
+                    copy.start()
+
+    answer(gy == 0)
     halves = cols // LANES
 
     def interleave(field):
@@ -328,12 +336,7 @@
     def _():
         walls[me] = back[gy]
 
-    @pl.when(first)
-    def _():
-        pl.semaphore_wait(ready, 2)
-        for k in range(CHUNKS):
-            for copy in x_copies(k):
-                copy.start()
+    answer(gy != 0)
 
     def substitute(k, carry):
         u, w = carry

time: 13.4 us -> 13 us (0.970)
  the two profiles are of different devices: /device:TPU:1 before, /device:TPU:0 now
where the time goes in v5:
time: 13 us; the launch traced here: 12.7 us
  Pallas kernels  12.1 us (93%)
  between operations  0.64 us (5%)
    pallas_call x1, Pallas kernels, local(): pl.pallas_call(functools.partial(kernel, sizes), out_shape=(jax.ShapeDtyp...  10.8 us
    pallas_call x1, Pallas kernels, local(): pl.pallas_call(write_out, out_shape=(jax.ShapeDtypeStruct(velocity.shape,...  1.27 us

profile of v5, /device:TPU:0, one launch (start us, length us, event | category | flops | bytes accessed | tf_op | source)
XLA Modules:
  0.0 12.7 jit_solution(7328283631078024459)
XLA Ops:
  0.6 10.8 %shard_map.68 = (f32[3,16,8,512]{3,2,1,0:T(8,128)S(1)}, f32[2,64,8,256]{3,2,1,0:T(8,128)S(1)}) custom-call(f32[3,16,8,512]{3,2,1,0:T(8,128)} %v_hbm.1, f32[2,64,8,256]{3,2,1,0:T(8,128)} %s_hbm.1, s32[8,512]{1,0:T(8,128)} %h_hbm.1, s32[16,8,512]{2,1,0:T(8,128)} %m_hbm.1, f32[8]{0:T(128)} %t_hbm.1), custom_call_target="tpu_custom_call" | custom-call | tf_op jit(solution)/shard_map/pallas_call | solution.py:537
  11.5 1.3 %shard_map.69 = (f32[3,16,8,512]{3,2,1,0:T(8,128)}, f32[2,64,8,256]{3,2,1,0:T(8,128)}) custom-call(f32[3,16,8,512]{3,2,1,0:T(8,128)S(1)} %get-tuple-element.4.advanced, f32[2,64,8,256]{3,2,1,0:T(8,128)S(1)} %get-tuple-element.5.fresh), custom_call_target="tpu_custom_call" | custom-call | tf_op jit(solution)/shard_map/pallas_call | solution.py:551

commit v6 on v5

--- a/solution.py
+++ b/solution.py
@@ -12,7 +12,8 @@
 LEVELS = 8
 LANES = 128
 MESH = pl.DeviceIdType.MESH
-CHUNKS = 4
+SIXTEENTHS = (16, 11, 6, 2, 0)
+CHUNKS = len(SIXTEENTHS) - 1
 
 time_step = 0.1
 viscosity = 0.02
@@ -40,7 +41,7 @@
     adv_ref, fresh_ref,
     v, s, h, mask, thrust_ref, tab_ref, eddy, coef_e, coef_f,
     xlo, xhi, zhalo, ypack_lo, ypack_hi, ylo, yhi,
-    stage, tops, back, walls, push,
+    stage, tops, back, walls, push, part,
     load_sem, x_send, x_recv, y_send, y_recv, z_send, z_recv, t_send, t_recv, w_send, w_recv, ready,
 ):
     n_gx, n_gy, n_gz, layers, rows, width, points, cols = sizes
@@ -52,6 +53,7 @@
     left, right = lax.rem(gx + n_gx - 1, n_gx), lax.rem(gx + 1, n_gx)
     below, above = lax.rem(gy + n_gy - 1, n_gy), lax.rem(gy + 1, n_gy)
     at_wall = gz == 0
+    cuts = [layers * sixteenth // 16 for sixteenth in SIXTEENTHS]
 
     loads = [
         pltpu.make_async_copy(h_hbm, h, load_sem.at[0]),
@@ -97,8 +99,7 @@
             tell(barrier, mate)
 
     def x_copies(k):
-        depth = layers // CHUNKS
-        zs = pl.ds((CHUNKS - 1 - k) * depth, depth)
+        zs = pl.ds(cuts[k + 1], cuts[k] - cuts[k + 1])
         to_right = pltpu.make_async_remote_copy(
             src_ref=v_hbm.at[:, zs, pl.ds(rows - 1, 1)], dst_ref=xlo.at[:, zs],
             send_sem=x_send.at[2 * k], recv_sem=x_recv.at[2 * k],
@@ -373,13 +374,11 @@
     row = lax.broadcasted_iota(jnp.int32, (rows, width), 0)
     col = lax.broadcasted_iota(jnp.int32, (rows, width), 1)
 
-    def layer(z, below_v, above_v, wall):
-        vel, xn, xp, yn, yp = [], [], [], [], []
+    def early(z, zp, zn):
+        vel, yn, yp = [], [], []
         for c in range(3):
             here = v[c, z]
             vel.append(here)
-            xp.append(jnp.where(row == 0, xlo[c, z], pltpu.roll(here, 1, 0)))
-            xn.append(jnp.where(row == rows - 1, xhi[c, z], pltpu.roll(here, rows - 1, 0)))
             slot = c * layers + z
             low = pltpu.roll(ylo[...], LANES - slot, 1)
             high = pltpu.roll(yhi[...], LANES - 1 - slot, 1)
@@ -387,51 +386,65 @@
             high = jnp.concatenate([high] * tiles, axis=1)
             yp.append(jnp.where(col == 0, low, pltpu.roll(here, 1, 1)))
             yn.append(jnp.where(col == width - 1, high, pltpu.roll(here, width - 1, 1)))
-        zn, zp = above_v, below_v
-        d_x = [xn[c] - xp[c] for c in range(3)]
         d_y = [yn[c] - yp[c] for c in range(3)]
         d_z = [zn[c] - zp[c] for c in range(3)]
-        diag = d_x[0] * d_x[0] + d_y[1] * d_y[1] + d_z[2] * d_z[2]
-        s_xy, s_xz, s_yz = d_y[0] + d_x[1], d_z[0] + d_x[2], d_z[1] + d_y[2]
-        cross = s_xy * s_xy + s_xz * s_xz + s_yz * s_yz
-        strain = jnp.sqrt(0.5 * diag + (0.25 * cross + 1e-06))
+        s_yz = d_z[1] + d_y[2]
+        part[0, z] = d_y[0]
+        part[1, z] = d_z[0]
+        part[2, z] = 0.5 * (d_y[1] * d_y[1] + d_z[2] * d_z[2]) + (0.25 * (s_yz * s_yz) + 1e-06)
+        for c in range(3):
+            part[3 + c, z] = (yn[c] + yp[c]) + (zn[c] + zp[c]) - 6.0 * vel[c]
+            flux = (yn[c] * yn[1] - yp[c] * yp[1]) + (zn[c] * zn[2] - zp[c] * zp[2])
+            kept = vel[c] - (0.5 * time_step) * flux
+            part[6 + c, z] = kept - push[z] if c == 2 else kept
+
+    def layer(z, wall):
+        xn, xp = [], []
+        for c in range(3):
+            here = v[c, z]
+            xp.append(jnp.where(row == 0, xlo[c, z], pltpu.roll(here, 1, 0)))
+            xn.append(jnp.where(row == rows - 1, xhi[c, z], pltpu.roll(here, rows - 1, 0)))
+        d_x = [xn[c] - xp[c] for c in range(3)]
+        s_xy, s_xz = part[0, z] + d_x[1], part[1, z] + d_x[2]
+        strain = jnp.sqrt(part[2, z] + (0.5 * (d_x[0] * d_x[0]) + 0.25 * (s_xy * s_xy + s_xz * s_xz)))
         viscous = time_step * viscosity + (time_step * smag_coeff) * strain
         for c in range(3):
-            total = (xn[c] + xp[c]) + (yn[c] + yp[c]) + (zn[c] + zp[c])
-            flux = (
-                (xn[c] * xn[0] - xp[c] * xp[0]) + (yn[c] * yn[1] - yp[c] * yp[1]) + (zn[c] * zn[2] - zp[c] * zp[2])
-            )
-            lap = total - 6.0 * vel[c]
+            lap = part[3 + c, z] + (xn[c] + xp[c])
             if wall is not None and c < 2:
-                lap = lap + wall[0] * vel[c]
-            out = vel[c] + (viscous * lap - (0.5 * time_step) * flux)
+                lap = lap + v[c, z]
+            out = part[6 + c, z] + (viscous * lap - (0.5 * time_step) * (xn[c] * xn[0] - xp[c] * xp[0]))
             if wall is not None and c < 2:
-                out = out - time_step * wall[1][c]
-            if c == 2:
-                out = out - push[z]
+                out = out - time_step * wall[c]
             adv_ref[c, z] = out
 
     def velocity_at(z):
         return [v[c, z] for c in range(3)]
+
+    bottom = at_wall.astype(jnp.float32)
+    early(layers - 1, velocity_at(layers - 2), [zhalo[c] * bottom for c in range(3)])
+    early(0, [zhalo[c] * (1.0 - bottom) for c in range(3)], velocity_at(1))
+
+    def early_inner(z, carry):
+        early(z, velocity_at(z - 1), velocity_at(z + 1))
+        return carry
+
+    lax.fori_loop(1, layers - 1, early_inner, 0)
 
     def x_wait(k):
         for copy in x_copies(k):
             copy.wait_recv()
 
-    depth = layers // CHUNKS
     x_wait(0)
-    bottom = at_wall.astype(jnp.float32)
-    layer(layers - 1, velocity_at(layers - 2), [zhalo[c] * bottom for c in range(3)], None)
+    layer(layers - 1, None)
 
     def inner(z, carry):
-        layer(z, velocity_at(z - 1), velocity_at(z + 1), None)
+        layer(z, None)
         return carry
 
-    lax.fori_loop(max(layers - depth, 1), layers - 1, inner, 0)
+    lax.fori_loop(max(cuts[1], 1), layers - 1, inner, 0)
     for k in range(1, CHUNKS):
         x_wait(k)
-        low = (CHUNKS - 1 - k) * depth
-        lax.fori_loop(max(low, 1), low + depth, inner, 0)
+        lax.fori_loop(max(cuts[k + 1], 1), cuts[k], inner, 0, unroll=2 if (cuts[k] - max(cuts[k + 1], 1)) % 2 == 0 else 1)
 
     def wall_wait(r):
         pltpu.make_async_remote_copy(
@@ -461,11 +474,11 @@
                         out = got if out is None else jnp.where(lane >= off, got, out)
                 parts.append(out)
             wall.append(jnp.concatenate(parts, axis=1))
-        layer(0, [jnp.zeros((rows, width), jnp.float32)] * 3, velocity_at(1), (1.0, wall))
+        layer(0, wall)
 
     @pl.when(jnp.logical_not(at_wall))
     def _():
-        layer(0, [zhalo[c] for c in range(3)], velocity_at(1), None)
+        layer(0, None)
 
     @pl.when(at_wall)
     def _():
@@ -525,6 +538,7 @@
         pltpu.VMEM((n_gy, 2, rows, LANES), f32),
         pltpu.VMEM((group, 2, rows, LANES), f32),
         pltpu.VMEM((layers, rows, width), f32),
+        pltpu.VMEM((9, layers, rows, width), f32),
         dma((7,)),
         dma((2 * CHUNKS,)), dma((2 * CHUNKS,)),
         dma((2,)), dma((2,)),

time: 13 us -> 12.1 us (0.931)
  Pallas kernels: 12.1 us -> 11.3 us
    pallas_call x1, Pallas kernels: 10.8 us -> 10 us  [local(): pl.pallas_call(functools.partial(kernel, sizes), out_shape=(jax.ShapeDtyp...]
where the time goes in v6:
time: 12.1 us; the launch traced here: 11.9 us
  Pallas kernels  11.3 us (93%)
  between operations  0.64 us (5%)
    pallas_call x1, Pallas kernels, local(): pl.pallas_call(functools.partial(kernel, sizes), out_shape=(jax.ShapeDtyp...  10 us
    pallas_call x1, Pallas kernels, local(): pl.pallas_call(write_out, out_shape=(jax.ShapeDtypeStruct(velocity.shape,...  1.27 us

profile of v6, /device:TPU:0, one launch (start us, length us, event | category | flops | bytes accessed | tf_op | source)
XLA Modules:
  0.0 11.9 jit_solution(10595367556216081002)
XLA Ops:
  0.6 10.0 %shard_map.68 = (f32[3,16,8,512]{3,2,1,0:T(8,128)S(1)}, f32[2,64,8,256]{3,2,1,0:T(8,128)S(1)}) custom-call(f32[3,16,8,512]{3,2,1,0:T(8,128)} %v_hbm.1, f32[2,64,8,256]{3,2,1,0:T(8,128)} %s_hbm.1, s32[8,512]{1,0:T(8,128)} %h_hbm.1, s32[16,8,512]{2,1,0:T(8,128)} %m_hbm.1, f32[8]{0:T(128)} %t_hbm.1), custom_call_target="tpu_custom_call" | custom-call | tf_op jit(solution)/shard_map/pallas_call | solution.py:551
  10.7 1.3 %shard_map.69 = (f32[3,16,8,512]{3,2,1,0:T(8,128)}, f32[2,64,8,256]{3,2,1,0:T(8,128)}) custom-call(f32[3,16,8,512]{3,2,1,0:T(8,128)S(1)} %get-tuple-element.4.advanced, f32[2,64,8,256]{3,2,1,0:T(8,128)S(1)} %get-tuple-element.5.fresh), custom_call_target="tpu_custom_call" | custom-call | tf_op jit(solution)/shard_map/pallas_call | solution.py:565
